TPU v7x, 512 devices: a whole 4x4x16 slice. The times are simulated.
512 devices in a mesh: vocab: 32 (over x, y, core), dp: 16 (over z).
Axes of the slice: x: 4, y: 4, z: 16, core: 2. Of those that a mesh axis runs over, the one named last changes fastest.
Arguments:
- hidden: bfloat16 [2048, 2048], P('dp', 'vocab')
- head_weight: bfloat16 [2048, 65536], P('dp', 'vocab')
- teacher_logits: bfloat16 [2048, 65536], P('dp', 'vocab')
- target_ids: int32 [2048], P('dp'), may hold values from 0 to 65535
- segment_ids: int32 [16, 128], P('dp'), may hold values from 0 to 15, never falling along the last dimension, each value on 1 to 16 neighbouring positions
- pair_order: int32 [16, 16], P('dp'), may hold values from 0 to 15, each once within a row
Outputs:
- hidden_grad: bfloat16 [2048, 2048], P('dp', 'vocab')
- head_grad: float32 [2048, 65536], P('dp', 'vocab')
- loss: float32 [], replicated
Inputs may be any that keep to these rules, and one draw needn't show every extreme that they name: `segment_ids`: in each group the row's sequence number never falls along the rows, and every sequence has 1 to 16 rows. `pair_order`: each group's row is a permutation of its 16 sequences; pair p is entry 2p (chosen) and entry 2p + 1 (rejected).
All inputs are finite; a program needn't handle non-finite values.
Results may differ from a plain program's by a relative error of at most 0.018.
Values may be sent and summed in bfloat16 or wider, within the bound.
No kernel may reach another device: no remote copies, remote signals or barrier semaphores. Data moves between devices by JAX's collectives and lax.ppermute only.
A program may use at most 64 MiB of HBM per device.

v0:
```python
import jax
import jax.numpy as jnp
from jax import lax
from jax.sharding import PartitionSpec as P

dpo_beta = 0.1
dpo_gamma = 4.0


def pair_weights(log_ratio, segments, ordering):
    seq_count = ordering.shape[0]
    labels = lax.broadcasted_iota(jnp.int32, (1, seq_count), 1)
    seq_hot = (segments[:, None] == labels).astype(jnp.float32)
    seq_ratio = jnp.sum(seq_hot * log_ratio[:, None], axis=0)
    chosen = ordering[0::2]
    rejected = ordering[1::2]
    chosen_hot = (chosen[:, None] == labels).astype(jnp.float32)
    rejected_hot = (rejected[:, None] == labels).astype(jnp.float32)
    margin = dpo_beta * (
        jnp.sum(chosen_hot * seq_ratio[None, :], axis=1)
        - jnp.sum(rejected_hot * seq_ratio[None, :], axis=1)
    )
    strength = dpo_gamma * dpo_beta * jax.nn.sigmoid(-margin)
    coeffs = jnp.sum((rejected_hot - chosen_hot) * strength[:, None], axis=0)
    row_weight = jnp.sum(seq_hot * coeffs[None, :], axis=1)
    return (row_weight, jnp.sum(jax.nn.softplus(-margin)))


def on_device(hidden, head_weight, teacher_logits, target_ids, segment_ids, pair_order):
    rows_full = lax.all_gather(hidden, "vocab", axis=1, tiled=True)
    weight_full = lax.all_gather(head_weight, "dp", axis=0, tiled=True)
    student = jnp.dot(rows_full, weight_full, preferred_element_type=jnp.float32)
    teacher = teacher_logits.astype(jnp.float32)
    shard_width = student.shape[1]
    offset = lax.axis_index("vocab") * shard_width
    column = lax.broadcasted_iota(jnp.int32, student.shape, 1) + offset
    is_target = column == target_ids[:, None]
    local_target = jnp.sum(jnp.where(is_target, student, 0.0), axis=1)
    local_tgt_teach = jnp.sum(jnp.where(is_target, teacher, 0.0), axis=1)
    local_max = jnp.max(student, axis=1)
    local_tmax = jnp.max(teacher, axis=1)
    max_student, max_teacher = lax.pmax((local_max, local_tmax), "vocab")
    exp_student = jnp.exp(student - max_student[:, None])
    exp_teacher = jnp.exp(teacher - max_teacher[:, None])
    sum_student, sum_teacher, cross, target_student, target_teacher = lax.psum(
        (
            jnp.sum(exp_student, axis=1),
            jnp.sum(exp_teacher, axis=1),
            jnp.sum(exp_teacher * (teacher - student), axis=1),
            local_target,
            local_tgt_teach,
        ),
        "vocab",
    )
    lse_student = max_student + jnp.log(sum_student)
    lse_teacher = max_teacher + jnp.log(sum_teacher)
    kl_rows = cross / sum_teacher - lse_teacher + lse_student
    log_ratio = target_student - lse_student - (target_teacher - lse_teacher)
    row_weight, dpo_sum = pair_weights(log_ratio, segment_ids[0], pair_order[0])
    group_objective = jnp.sum(kl_rows) + dpo_gamma * dpo_sum
    summed_objective = lax.psum(group_objective, "dp")
    loss_value = summed_objective / (rows_full.shape[0] * lax.axis_size("dp"))
    prob_student = exp_student / sum_student[:, None]
    prob_teacher = exp_teacher / sum_teacher[:, None]
    logit_grad = (
        prob_student
        - prob_teacher
        + row_weight[:, None] * (is_target.astype(jnp.float32) - prob_student)
    ).astype(jnp.bfloat16)
    hidden_term = lax.dot_general(
        logit_grad, weight_full, (((1,), (1,)), ((), ())), preferred_element_type=jnp.float32
    )
    hidden_grad = lax.psum_scatter(
        hidden_term.astype(jnp.bfloat16), "vocab", scatter_dimension=1, tiled=True
    )
    grad_cols = lax.all_to_all(rows_full, "dp", split_axis=1, concat_axis=0, tiled=True)
    head_grad = lax.dot_general(
        grad_cols,
        lax.all_gather(logit_grad, "dp", axis=0, tiled=True),
        (((0,), (0,)), ((), ())),
        preferred_element_type=jnp.float32,
    )
    return (hidden_grad, head_grad, loss_value)


def solution(mesh):
    return jax.shard_map(
        on_device,
        mesh=mesh,
        in_specs=(
            P("dp", "vocab"),
            P("dp", "vocab"),
            P("dp", "vocab"),
            P("dp"),
            P("dp", None),
            P("dp", None),
        ),
        out_specs=(P("dp", "vocab"), P("dp", "vocab"), P()),
        check_vma=False,
    )
```

profile of v0, /device:TPU:2, one launch (start us, length us, event | category | flops | bytes accessed | tf_op | source)
XLA Modules:
  0.0 486.9 jit_solution(1537256044486397161)
XLA Ops:
  7.2 0.0 all-gather.3.cloned.1.call-start
  7.2 0.7 all-gather.3.cloned.1.call-update
  7.9 0.0 copy-start
  7.9 0.0 all-gather.5.cloned.1.call-start
  8.0 0.8 slice.7
  8.8 0.7 slice.6
  9.5 1.2 reduce_max.24
  10.7 29.9 %all_gather.9 = bf16[128,2048]{0,1:T(8,128)(2,1)} all-gather(bf16[128,64]{0,1:T(8,128)(2,1)} %param.6), channel_id=1, replica_groups=mesh['vocab'=32,'dp'=16] {'vocab'}, dimensions={1}, use_global_device_ids=true | all-gather | bytes 540672 | tf_op jit(solution)/shard_map/all_gather | solution.py:30
  40.6 79.9 %all-gather.3.cloned.1.call-done = bf16[2048,2048]{1,0:T(8,128)(2,1)} async-done(((bf16[128,2048]{1,0:T(8,128)(2,1)}), bf16[2048,2048]{1,0:T(8,128)(2,1)}) %all-gather.3.cloned.1.call-update) | async-done | bytes 8388624 | tf_op jit(solution)/shard_map/all_gather | solution.py:31
  120.5 4.9 %fusion.14 = (f32[128]{0:T(128)S(1)}, f32[128,2048]{1,0:T(8,128)S(1)}) fusion(bf16[128,2048]{0,1:T(8,128)(2,1)} %all_gather.9, bf16[2048,2048]{1,0:T(8,128)(2,1)} %all-gather.3.cloned.1.call-done), kind=kOutput, calls=%fused_computation.38 | convolution fusion | flops 1074003840 | bytes 9961984 | tf_op jit(solution)/shard_map/dot_general | solution.py:32
  125.4 56.2 %all-reduce.1 = (f32[128]{0:T(128)S(1)}, f32[128]{0:T(128)S(1)}) all-reduce(bf16[128]{0:T(256)(128)(2,1)S(1)} %reduce_max.24, f32[128]{0:T(128)S(1)} %get-tuple-element.33), channel_id=1, replica_groups=mesh['vocab'=32,'dp'=16] {'vocab'}, use_global_device_ids=true, to_apply=%region_5.6 | all-reduce | flops 256 | bytes 1792 | tf_op jit(solution)/shard_map/pmax | solution.py:42
  181.6 0.8 fusion.6
  182.4 56.8 %all-reduce = (f32[128]{0:T(128)S(1)}, f32[128]{0:T(128)S(1)}, f32[128]{0:T(128)S(1)}, f32[128]{0:T(128)S(1)}, f32[128]{0:T(128)S(1)}) all-reduce(f32[128]{0:T(128)S(1)} %get-tuple-element.18, f32[128]{0:T(128)S(1)} %get-tuple-element.16, f32[128]{0:T(128)S(1)} %get-tuple-element.19, ...), channel_id=1, replica_groups=mesh['vocab'=32,'dp'=16] {'vocab'}, use_global_device_ids=true, to_apply=%region_11.12 | all-reduce | flops 640 | bytes 5120 | tf_op jit(solution)/shard_map/psum | solution.py:45
  239.2 0.6 add_reduce_fusion
  239.9 0.1 select_reduce_fusion.1
  240.0 0.2 select_reduce_fusion.2
  240.2 0.6 fusion.13
  240.8 0.1 multiply_reduce_fusion
  240.9 0.1 select_reduce_fusion
  241.0 1.4 fusion.11
  242.4 0.0 all-gather.5.cloned.1.call-update
  242.4 8.9 %all-to-all-start = ((bf16[128,16,128]{0,2,1:T(8,128)(2,1)}), bf16[128,16,128]{0,2,1:T(8,128)(2,1)S(1)}, u32[]{:S(2)}, u32[]{:S(2)}) async-start(bf16[128,16,128]{0,2,1:T(8,128)(2,1)} %bitcast.2), calls=%async_computation.1 | async-start | bytes 1048576 | tf_op jit(solution)/shard_map/all_to_all | solution.py:76
  251.3 0.0 reduce-scatter.2.cloned.1.call-start
  251.4 6.7 %convolution_convert_fusion = bf16[128,2048]{0,1:T(8,128)(2,1)} fusion(bf16[128,2048]{1,0:T(8,128)(2,1)} %fusion.11, bf16[2048,2048]{1,0:T(8,128)(2,1)} %all-gather.3.cloned.1.call-done), kind=kOutput, calls=%fused_computation.1 | convolution fusion | flops 1074003968 | bytes 9437184 | tf_op jit(solution)/shard_map/dot_general | solution.py:70
  258.1 0.0 reduce-scatter.2.cloned.1.call-update
  259.3 21.5 %all-to-all-done = bf16[128,16,128]{0,2,1:T(8,128)(2,1)S(1)} async-done(((bf16[128,16,128]{0,2,1:T(8,128)(2,1)}), bf16[128,16,128]{0,2,1:T(8,128)(2,1)S(1)}, u32[]{:S(2)}, u32[]{:S(2)}) %all-to-all-start) | async-done | bytes 524320 | tf_op jit(solution)/shard_map/all_to_all | solution.py:76
  280.9 0.3 copy.13
  281.1 32.6 %psum.47 = f32[]{:T(128)} all-reduce(f32[]{:T(128)S(6)} %add.55), channel_id=1, replica_groups=mesh['vocab'=32,'dp'=16] {'dp'}, use_global_device_ids=true, to_apply=%region_22.23 | all-reduce | flops 1 | bytes 8 | tf_op jit(solution)/shard_map/psum | solution.py:61
  314.4 48.8 %all-gather.5.cloned.1.call-done = bf16[2048,2048]{1,0:T(8,128)(2,1)} async-done(((bf16[128,2048]{1,0:T(8,128)(2,1)}), bf16[2048,2048]{1,0:T(8,128)(2,1)}) %all-gather.5.cloned.1.call-update) | async-done | bytes 8388624 | tf_op jit(solution)/shard_map/all_gather | solution.py:79
  363.2 5.8 %convolution_bitcast_fusion = f32[128,2048]{0,1:T(8,128)S(1)} fusion(bf16[2048,2048]{1,0:T(8,128)(2,1)} %all-gather.5.cloned.1.call-done, bf16[2048,128]{1,0:T(8,128)(2,1)S(1)} %bitcast.14), kind=kOutput, calls=%fused_computation | convolution fusion | flops 1073741824 | bytes 9961472 | tf_op jit(solution)/shard_map/dot_general | solution.py:77
  369.0 1.3 copy.14
  370.3 109.0 %reduce-scatter.2.cloned.1.call-done = bf16[128,64]{0,1:T(8,128)(2,1)} async-done(((bf16[128,2048]{0,1:T(8,128)(2,1)}), bf16[128,64]{0,1:T(8,128)(2,1)}) %reduce-scatter.2.cloned.1.call-update) | async-done | bytes 16400 | tf_op jit(solution)/shard_map/reduce_scatter | solution.py:73
  (6 shorter events, 0.0 us)
Async XLA Ops:
  7.2 113.3 %all-gather.3.cloned.1.call-start = ((), (), s32[]{:S(2)}) async-start(), calls=%async_computation.2 | async-start | bytes 8912896 | tf_op jit(solution)/shard_map/all_gather | solution.py:31
  7.9 173.7 %copy-start = (bf16[128,2048]{1,0:T(8,128)(2,1)S(1)}, bf16[128,2048]{1,0:T(8,128)(2,1)}, u32[]{:S(2)}) copy-start(bf16[128,2048]{1,0:T(8,128)(2,1)} %param.8) | copy-start | bytes 1572868
  7.9 173.7 %copy-start.1 = (s32[128]{0:T(128)S(1)}, s32[128]{0:T(128)}, u32[]{:S(2)}) copy-start(s32[128]{0:T(128)} %param.9) | copy-start | bytes 1540
  7.9 355.3 %all-gather.5.cloned.1.call-start = ((), (), s32[]{:S(2)}) async-start(), calls=%async_computation.4 | async-start | bytes 8912896 | tf_op jit(solution)/shard_map/all_gather | solution.py:79
  40.6 199.2 %copy-start.2 = (s32[1,128]{1,0:T(1,128)S(1)}, s32[1,128]{1,0:T(1,128)}, u32[]{:S(2)}) copy-start(s32[1,128]{1,0:T(1,128)} %param.10) | copy-start | bytes 1540
  242.4 38.4 %all-to-all-start = ((bf16[128,16,128]{0,2,1:T(8,128)(2,1)}), bf16[128,16,128]{0,2,1:T(8,128)(2,1)S(1)}, u32[]{:S(2)}, u32[]{:S(2)}) async-start(bf16[128,16,128]{0,2,1:T(8,128)(2,1)} %bitcast.2), calls=%async_computation.1 | async-start | bytes 1048576 | tf_op jit(solution)/shard_map/all_to_all | solution.py:76
  251.3 227.9 %reduce-scatter.2.cloned.1.call-start = ((), (), s32[]{:S(2)}) async-start(), calls=%async_computation.3 | async-start | bytes 540672 | tf_op jit(solution)/shard_map/reduce_scatter | solution.py:73
Sparse Core Ops, SparseCore 0:
  10.1 110.3 all-gather.2
  242.6 120.6 all-gather.4
  368.1 111.0 reduce-scatter.1
where the time goes:
time: 487 us
  waiting for transfers between devices  260 us (53%)
  blocking collectives  175 us (36%)
  matrix products  17.4 us (4%)
  between operations  16.8 us (3%)
  starting transfers between devices  9 us (2%)
  other arithmetic  5.2 us (1%)
    reduce_scatter x1, waiting for transfers between devices, on_device(): lax.psum_scatter(hidden_term.astype(jnp.bfloat16), 'vocab', scatter_dimen...  109 us
    all_gather x1, waiting for transfers between devices, on_device(): weight_full = lax.all_gather(head_weight, 'dp', axis=0, tiled=True)  79.9 us
    psum x1, blocking collectives, on_device(): lax.psum((jnp.sum(exp_student, axis=1), jnp.sum(exp_teacher, axis=1), jnp...  56.8 us
    pmax x1, blocking collectives, on_device(): max_student, max_teacher = lax.pmax((local_max, local_tmax), 'vocab')  56.2 us
    all_gather x1, waiting for transfers between devices, on_device(): lax.all_gather(logit_grad, 'dp', axis=0, tiled=True)  48.8 us
    psum x1, blocking collectives, on_device(): summed_objective = lax.psum(group_objective, 'dp')  32.6 us
    all_gather x1, blocking collectives, on_device(): rows_full = lax.all_gather(hidden, 'vocab', axis=1, tiled=True)  29.9 us
    all_to_all x1, waiting for transfers between devices, on_device(): lax.all_to_all(rows_full, 'dp', split_axis=1, concat_axis=0, tiled=True)  21.5 us
  transfers between devices with their start and end apart: 4, of which 4 were waited for; matrix products, arithmetic and copies ran while one was open for 3% of the time, Pallas kernels for 0%

commit v1 on v0

--- a/solution.py
+++ b/solution.py
@@ -73,7 +73,15 @@
     hidden_grad = lax.psum_scatter(
         hidden_term.astype(jnp.bfloat16), "vocab", scatter_dimension=1, tiled=True
     )
-    grad_cols = lax.all_to_all(rows_full, "dp", split_axis=1, concat_axis=0, tiled=True)
+    grad_cols = jnp.concatenate(
+        lax.all_to_all(
+            jnp.stack(jnp.split(rows_full, lax.psum(1, axis_name="dp"), axis=1)),
+            axis_name="dp",
+            split_axis=0,
+            concat_axis=0,
+        ),
+        axis=0,
+    )
     head_grad = lax.dot_general(
         grad_cols,
         lax.all_gather(logit_grad, "dp", axis=0, tiled=True),

time: 487 us -> 493 us (1.012)
  waiting for transfers between devices: 260 us -> 244 us
  blocking collectives: 175 us -> 187 us
  local copies, waits for them, and re-layouts: 3.14 us -> 13.2 us
    all_to_all x1, waiting for transfers between devices: 21.5 us -> 0.01 us  [on_device(): lax.all_to_all(jnp.stack(jnp.split(rows_full, lax.psum(1, axis_name='dp')...]
    psum x1, blocking collectives: 32.6 us -> 46 us  [on_device(): summed_objective = lax.psum(group_objective, 'dp')]
    unnamed x7 -> x37, local copies, waits for them, and re-layouts: 1.32 us -> 11 us
    all_gather x1, waiting for transfers between devices: 48.8 us -> 57.2 us  [on_device(): lax.all_gather(logit_grad, 'dp', axis=0, tiled=True)]
  transfers between devices with their start and end apart: 4 -> 4, of which waited for: 4 -> 3; matrix products, arithmetic and copies ran while one was open for 3% -> 5% of each run, Pallas kernels for 0% -> 0%
where the time goes in v1:
time: 493 us; the launch traced here: 492 us
  waiting for transfers between devices  244 us (49%)
  blocking collectives  187 us (38%)
  matrix products  17.1 us (3%)
  between operations  16.9 us (3%)
  local copies, waits for them, and re-layouts  13.2 us (3%)
  starting transfers between devices  8.99 us (2%)
  other arithmetic  5.18 us (1%)
    reduce_scatter x1, waiting for transfers between devices, on_device(): lax.psum_scatter(hidden_term.astype(jnp.bfloat16), 'vocab', scatter_dimen...  104 us
    all_gather x1, waiting for transfers between devices, on_device(): weight_full = lax.all_gather(head_weight, 'dp', axis=0, tiled=True)  82.1 us
    all_gather x1, waiting for transfers between devices, on_device(): lax.all_gather(logit_grad, 'dp', axis=0, tiled=True)  57.2 us
    psum x1, blocking collectives, on_device(): lax.psum((jnp.sum(exp_student, axis=1), jnp.sum(exp_teacher, axis=1), jnp...  56.8 us
    pmax x1, blocking collectives, on_device(): max_student, max_teacher = lax.pmax((local_max, local_tmax), 'vocab')  56.2 us
    psum x1, blocking collectives, on_device(): summed_objective = lax.psum(group_objective, 'dp')  46 us
    all_gather x1, blocking collectives, on_device(): rows_full = lax.all_gather(hidden, 'vocab', axis=1, tiled=True)  27.6 us
    unnamed x37, local copies, waits for them, and re-layouts  11 us
  transfers between devices with their start and end apart: 4, of which 3 were waited for; matrix products, arithmetic and copies ran while one was open for 5% of the time, Pallas kernels for 0%

profile of v1, /device:TPU:2, one launch (start us, length us, event | category | flops | bytes accessed | tf_op | source)
XLA Modules:
  0.0 492.2 jit_solution(2252001102127599739)
XLA Ops:
  7.2 0.7 all-gather.3.cloned.1.call-update
  8.0 0.8 slice.7
  8.8 0.7 slice.6
  9.5 1.2 reduce_max.24
  10.7 27.6 %all_gather.9 = bf16[128,2048]{0,1:T(8,128)(2,1)S(1)} all-gather(bf16[128,64]{0,1:T(8,128)(2,1)} %param.6), channel_id=1, replica_groups=mesh['vocab'=32,'dp'=16] {'vocab'}, dimensions={1}, use_global_device_ids=true | all-gather | bytes 540672 | tf_op jit(solution)/shard_map/all_gather | solution.py:30
  38.4 82.1 %all-gather.3.cloned.1.call-done = bf16[2048,2048]{1,0:T(8,128)(2,1)} async-done(((bf16[128,2048]{1,0:T(8,128)(2,1)}), bf16[2048,2048]{1,0:T(8,128)(2,1)}) %all-gather.3.cloned.1.call-update) | async-done | bytes 8388624 | tf_op jit(solution)/shard_map/all_gather | solution.py:31
  120.5 4.7 fusion.15
  125.2 56.2 %all-reduce.1 = (f32[128]{0:T(128)S(1)}, f32[128]{0:T(128)S(1)}) all-reduce(bf16[128]{0:T(256)(128)(2,1)S(1)} %reduce_max.24, f32[128]{0:T(128)S(1)} %get-tuple-element.37), channel_id=1, replica_groups=mesh['vocab'=32,'dp'=16] {'vocab'}, use_global_device_ids=true, to_apply=%region_5.6 | all-reduce | flops 256 | bytes 1792 | tf_op jit(solution)/shard_map/pmax | solution.py:42
  181.4 0.8 fusion.6
  182.2 56.8 %all-reduce = (f32[128]{0:T(128)S(1)}, f32[128]{0:T(128)S(1)}, f32[128]{0:T(128)S(1)}, f32[128]{0:T(128)S(1)}, f32[128]{0:T(128)S(1)}) all-reduce(f32[128]{0:T(128)S(1)} %get-tuple-element.6, f32[128]{0:T(128)S(1)} %get-tuple-element.4, f32[128]{0:T(128)S(1)} %get-tuple-element.7, ...), channel_id=1, replica_groups=mesh['vocab'=32,'dp'=16] {'vocab'}, use_global_device_ids=true, to_apply=%region_11.12 | all-reduce | flops 640 | bytes 5120 | tf_op jit(solution)/shard_map/psum | solution.py:45
  239.0 0.6 add_reduce_fusion
  240.0 0.6 fusion.13
  240.8 1.4 fusion.11
  244.3 0.6 constant_dynamic-update-slice_fusion.15
  244.9 0.6 constant_dynamic-update-slice_fusion.14
  245.5 0.6 constant_dynamic-update-slice_fusion.13
  246.1 0.6 constant_dynamic-update-slice_fusion.12
  246.7 0.6 constant_dynamic-update-slice_fusion.11
  247.3 0.6 constant_dynamic-update-slice_fusion.10
  247.9 0.6 constant_dynamic-update-slice_fusion.9
  248.5 0.6 constant_dynamic-update-slice_fusion.8
  250.3 0.6 constant_dynamic-update-slice_fusion.5
  250.9 0.6 constant_dynamic-update-slice_fusion.4
  252.2 0.6 constant_dynamic-update-slice_fusion.2
  252.8 0.6 constant_dynamic-update-slice_fusion.1
  253.4 0.6 constant_dynamic-update-slice_fusion
  254.0 8.9 %all-to-all-start = ((bf16[16,128,128]{2,1,0:T(8,128)(2,1)}), bf16[16,128,128]{2,1,0:T(8,128)(2,1)S(1)}, u32[]{:S(2)}, u32[]{:S(2)}) async-start(bf16[16,128,128]{2,1,0:T(8,128)(2,1)} %constant_dynamic-update-slice_fusion), calls=%async_computation.1 | async-start | bytes 1048576 | tf_op jit(solution)/shard_map/all_to_all | solution.py:77
  262.9 6.7 %convolution_convert_fusion = bf16[128,2048]{0,1:T(8,128)(2,1)} fusion(bf16[128,2048]{1,0:T(8,128)(2,1)} %fusion.11, bf16[2048,2048]{1,0:T(8,128)(2,1)} %all-gather.3.cloned.1.call-done), kind=kOutput, calls=%fused_computation | convolution fusion | flops 1074003968 | bytes 9437184 | tf_op jit(solution)/shard_map/dot_general | solution.py:70
  270.9 46.0 %psum.47 = f32[]{:T(128)} all-reduce(f32[]{:T(128)S(6)} %add.55), channel_id=1, replica_groups=mesh['vocab'=32,'dp'=16] {'dp'}, use_global_device_ids=true, to_apply=%region_22.23 | all-reduce | flops 1 | bytes 8 | tf_op jit(solution)/shard_map/psum | solution.py:61
  317.5 57.2 %all-gather.5.cloned.1.call-done = bf16[2048,2048]{1,0:T(8,128)(2,1)} async-done(((bf16[128,2048]{1,0:T(8,128)(2,1)}), bf16[2048,2048]{1,0:T(8,128)(2,1)}) %all-gather.5.cloned.1.call-update) | async-done | bytes 8388624 | tf_op jit(solution)/shard_map/all_gather | solution.py:87
  374.7 5.6 %fusion.16 = f32[128,2048]{1,0:T(8,128)} fusion(bf16[2048,128]{1,0:T(8,128)(2,1)S(1)} %bitcast.41, bf16[2048,2048]{1,0:T(8,128)(2,1)} %all-gather.5.cloned.1.call-done), kind=kOutput, calls=%fused_computation.55 | convolution fusion | flops 1073741824 | bytes 9961472 | tf_op jit(solution)/shard_map/dot_general | solution.py:85
  380.4 104.2 %reduce-scatter.2.cloned.1.call-done = bf16[128,64]{0,1:T(8,128)(2,1)} async-done(((bf16[128,2048]{0,1:T(8,128)(2,1)}), bf16[128,64]{0,1:T(8,128)(2,1)}) %reduce-scatter.2.cloned.1.call-update) | async-done | bytes 16400 | tf_op jit(solution)/shard_map/reduce_scatter | solution.py:73
  (37 shorter events, 4.4 us)
Async XLA Ops:
  7.2 113.3 %all-gather.3.cloned.1.call-start = ((), (), s32[]{:S(2)}) async-start(), calls=%async_computation.2 | async-start | bytes 8912896 | tf_op jit(solution)/shard_map/all_gather | solution.py:31
  7.9 173.5 %copy-start = (bf16[128,2048]{1,0:T(8,128)(2,1)S(1)}, bf16[128,2048]{1,0:T(8,128)(2,1)}, u32[]{:S(2)}) copy-start(bf16[128,2048]{1,0:T(8,128)(2,1)} %param.8) | copy-start | bytes 1572868
  7.9 173.5 %copy-start.1 = (s32[128]{0:T(128)S(1)}, s32[128]{0:T(128)}, u32[]{:S(2)}) copy-start(s32[128]{0:T(128)} %param.9) | copy-start | bytes 1540
  7.9 366.8 %all-gather.5.cloned.1.call-start = ((), (), s32[]{:S(2)}) async-start(), calls=%async_computation.4 | async-start | bytes 8912896 | tf_op jit(solution)/shard_map/all_gather | solution.py:87
  38.4 201.3 %copy-start.2 = (s32[1,128]{1,0:T(1,128)S(1)}, s32[1,128]{1,0:T(1,128)}, u32[]{:S(2)}) copy-start(s32[1,128]{1,0:T(1,128)} %param.10) | copy-start | bytes 1540
  254.0 63.6 %all-to-all-start = ((bf16[16,128,128]{2,1,0:T(8,128)(2,1)}), bf16[16,128,128]{2,1,0:T(8,128)(2,1)S(1)}, u32[]{:S(2)}, u32[]{:S(2)}) async-start(bf16[16,128,128]{2,1,0:T(8,128)(2,1)} %constant_dynamic-update-slice_fusion), calls=%async_computation.1 | async-start | bytes 1048576 | tf_op jit(solution)/shard_map/all_to_all | solution.py:77
  262.9 221.7 %reduce-scatter.2.cloned.1.call-start = ((), (), s32[]{:S(2)}) async-start(), calls=%async_computation.3 | async-start | bytes 540672 | tf_op jit(solution)/shard_map/reduce_scatter | solution.py:73
Sparse Core Ops, SparseCore 0:
  10.1 110.3 all-gather.2
  242.4 132.3 all-gather.4
  379.6 104.8 reduce-scatter.1
